TPU v7x, 32 devices: a whole 2x2x4 slice. The times are simulated.
32 devices in a mesh: band: 2 (over y), inp: 4 (over z), slab: 2 (over x), pol: 2 (over core).
Axes of the slice: x: 2, y: 2, z: 4, core: 2. Of those that a mesh axis runs over, the one named last changes fastest.
Arguments:
- voltage: bfloat16 [4, 1024, 32768], P('band', ('inp', 'pol'), 'slab'), parts along dimension 0, may hold values from -8 to 7, as said below
- filter_taps: int32 [4, 512], replicated, may hold values from -128 to 127
Outputs:
- visibility: float32 [4, 64, 1024, 1024], P('band', 'slab', ('inp', 'pol')), parts along dimension 0
There are 2 independent parts, one for each index of `band`. A program takes and returns all parts, laid end to end along the dimension named above; an argument that names none is the same for every part. Nothing has to cross between parts.
Inputs may be any that keep to these rules, and one draw needn't show every extreme that they name: `voltage`: every entry is a whole number.
All inputs are finite; a program needn't handle non-finite values.
Results may differ from a plain program's by a relative error of at most 0.0035.
Values may be sent and summed in bfloat16 or wider, within the bound.
A program may use at most 320 MiB of HBM per device.

v0:
```python
import math

import jax
import jax.numpy as jnp
from jax import lax
from jax.sharding import PartitionSpec as P

CHANNELS = 64


def passed_along(value, axis, steps):
    count = lax.axis_size(axis)
    first, last = (max(0, -steps), min(count, count - steps))
    return lax.ppermute(value, axis, [(source, source + steps) for source in range(first, last)])


def dft_table(channel_count, points):
    channel = jnp.arange(channel_count, dtype=jnp.int32)[:, None]
    sample = jnp.arange(points, dtype=jnp.int32)[None, :]
    residue = channel * sample % points
    angles = residue.astype(jnp.float32) * (2.0 * math.pi / points)
    cosine = jnp.cos(angles) / 32.0
    sine_part = jnp.sin(angles) / 32.0
    real_rows = jnp.stack([cosine, sine_part], axis=1)
    imag_rows = jnp.stack([-sine_part, cosine], axis=1)
    return jnp.stack([real_rows, imag_rows], axis=0).astype(jnp.bfloat16)


def filter_bank(voltage, filter_taps, tail_rows):
    tap_count = filter_taps.shape[0]
    points = filter_taps.shape[1]
    extended = jnp.concatenate([tail_rows, voltage], axis=2).astype(jnp.float32)
    spectra_here = voltage.shape[2] // points
    frames = extended.reshape(2, voltage.shape[1], spectra_here + tap_count - 1, points)
    weights = filter_taps.astype(jnp.float32) / 128.0
    filtered = weights[0] * frames[:, :, 0:spectra_here]
    for tap_index in range(1, tap_count):
        filtered = (
            filtered + weights[tap_index] * frames[:, :, tap_index : tap_index + spectra_here]
        )
    return filtered.astype(jnp.bfloat16)


def accumulate(left_rows, incoming):
    row_count = left_rows.shape[1] // 2
    col_count = incoming.shape[2]
    right_rows = incoming.reshape(incoming.shape[0], 2 * col_count, incoming.shape[3])
    products = jnp.einsum("fis,fjs->fij", left_rows, right_rows, preferred_element_type=jnp.float32)
    real_part = products[:, :row_count, :col_count] + products[:, row_count:, col_count:]
    imag_part = products[:, row_count:, :col_count] - products[:, :row_count, col_count:]
    update = jnp.stack([real_part, imag_part], axis=0)
    return update


def make_step(turned, incoming):
    left_rows = turned.reshape(turned.shape[0], 2 * turned.shape[2], turned.shape[3])
    return accumulate(left_rows, incoming)


def body(voltage, filter_taps):
    points = filter_taps.shape[1]
    tail_length = (filter_taps.shape[0] - 1) * points
    tail_rows = passed_along(voltage[:, :, voltage.shape[2] - tail_length :], "slab", 1)
    filtered = filter_bank(voltage, filter_taps, tail_rows)
    spectra = jnp.einsum(
        "afbp,bisp->fais", dft_table(CHANNELS, points), filtered, preferred_element_type=jnp.float32
    ).astype(jnp.bfloat16)
    turned = lax.all_to_all(spectra, "slab", split_axis=0, concat_axis=3, tiled=True)
    partial_value = make_step(turned, lax.all_gather(turned, ("inp", "pol"), axis=2, tiled=True))
    return partial_value / (32.0 * turned.shape[3])


def solution(mesh):
    placed = (P("band", ("inp", "pol"), "slab"), P())
    return jax.shard_map(
        body,
        mesh=mesh,
        in_specs=placed,
        out_specs=P("band", "slab", ("inp", "pol"), None),
        check_vma=False,
    )
```

profile of v0, /device:TPU:0, one launch (start us, length us, event | category | flops | bytes accessed | tf_op | source)
XLA Modules:
  0.0 289.4 jit_solution(14646888987016928391)
XLA Ops:
  6.5 0.0 copy-start
  6.5 0.0 all-gather.2.cloned.1.call-start
  6.5 11.9 %copy.20 = bf16[2,128,16384]{1,2,0:T(8,128)(2,1)} copy(bf16[2,128,16384]{2,1,0:T(8,128)(2,1)} %param.2) | data formatting | bytes 16777216 | tf_op args[0]
  18.5 1.2 slice.53
  19.6 4.9 %collective-permute-start = (bf16[2,128,1536]{1,2,0:T(8,128)(2,1)S(1)}, bf16[2,128,1536]{1,2,0:T(8,128)(2,1)S(1)}, u32[]{:S(2)}, u32[]{:S(2)}) collective-permute-start(bf16[2,128,1536]{1,2,0:T(8,128)(2,1)S(1)} %slice.53), channel_id=1, source_target_pairs={{0,2},{1,3},{4,6},{5,7},{8,10},{9,11},{12,14},{13,15},{16,18},{17,... | collective-permute-start | bytes 2359304 | tf_op jit(solution)/shard_map/ppermute | solution.py:14
  24.5 0.5 fusion.22
  25.0 0.5 negate_convert_fusion
  25.6 0.0 copy-done
  25.7 15.6 %collective-permute-done = bf16[2,128,1536]{1,2,0:T(8,128)(2,1)S(1)} collective-permute-done((bf16[2,128,1536]{1,2,0:T(8,128)(2,1)S(1)}, bf16[2,128,1536]{1,2,0:T(8,128)(2,1)S(1)}, u32[]{:S(2)}, u32[]{:S(2)}) %collective-permute-start) | collective-permute-done | bytes 786464 | tf_op jit(solution)/shard_map/ppermute | solution.py:14
  41.3 10.6 %pad_maximum_fusion = bf16[2,128,17920]{1,2,0:T(8,128)(2,1)} fusion(bf16[2,128,16384]{1,2,0:T(8,128)(2,1)} %copy.20, bf16[2,128,1536]{1,2,0:T(8,128)(2,1)S(1)} %collective-permute-done), kind=kLoop, calls=%fused_computation.13 | loop fusion | flops 18350080 | bytes 18350080 | tf_op jit(solution)/shard_map/concatenate | solution.py:32
  51.9 12.8 %convert.20 = f32[2,128,35,512]{1,3,2,0:T(8,128)} convert(bf16[2,128,35,512]{1,3,2,0:T(8,128)(2,1)} %bitcast.39) | non-fusion elementwise | flops 4587520 | bytes 27525120 | tf_op jit(solution)/shard_map/convert_element_type | solution.py:32
  64.6 22.1 %fusion.11 = bf16[64,2,128,32]{2,0,1,3:T(8,128)(2,1)S(1)} fusion(bf16[1,64,2,512]{3,1,2,0:T(8,128)(2,1)S(1)} %get-tuple-element.8, bf16[1,64,2,512]{3,1,2,0:T(8,128)(2,1)S(1)} %get-tuple-element.7, f32[2,128,35,512]{1,3,2,0:T(8,128)} %convert.20, f32[512]{0:T(512)S(1)} %bitcast.45, f32[512]{0:T(512)S(1)} %bitcast.46, f32[512]{0:T(512)S(1)} %bitcast.47, ...), kind=kOutput, calls=%fused_computation.18 | convolution fusion | flops 1108344832 | bytes 68427776 | tf_op jit(solution)/shard_map/afbp,bisp->fais/dot_general | solution.py:65
  86.7 1.1 copy.23
  87.8 16.4 %all_to_all.18 = bf16[64,2,128,32]{2,1,3,0:T(2,128)(2,1)S(1)} all-to-all(bf16[64,2,128,32]{2,1,3,0:T(2,128)(2,1)S(1)} %copy.23), channel_id=1, replica_groups=mesh['band'=2,'inp'=4,'slab'=2,'pol'=2] {'slab'}, dimensions={0} | all-to-all | bytes 2097152 | tf_op jit(solution)/shard_map/all_to_all | solution.py:68
  104.2 0.2 copy.24
  104.4 1.1 copy.26
  105.6 0.0 all-gather.2.cloned.1.call-update
  105.6 1.1 copy.25
  106.7 0.7 reshape.96
  107.4 81.2 %all-gather.2.cloned.1.call-done = bf16[32,2,1024,64]{2,3,1,0:T(8,128)(2,1)} async-done(((bf16[32,2,128,64]{2,3,1,0:T(8,128)(2,1)}), bf16[32,2,1024,64]{2,3,1,0:T(8,128)(2,1)}) %all-gather.2.cloned.1.call-update) | async-done | bytes 8388624 | tf_op jit(solution)/shard_map/all_gather | solution.py:69
  188.6 8.3 %copy.32 = bf16[32,2,8,8,1024]{4,3,1,2,0:T(8,128)(2,1)} copy(bf16[32,2,8,8,1024]{4,3,2,1,0:T(8,128)(2,1)} %bitcast.42) | data formatting | bytes 16777216 | tf_op jit(solution)/shard_map/reshape | solution.py:47
  196.9 26.8 %fusion.25 = f32[32,256,2048]{2,1,0:T(8,128)} fusion(bf16[32,256,64]{1,2,0:T(8,128)(2,1)S(1)} %reshape.96, bf16[32,2048,64]{1,2,0:T(8,128)(2,1)} %bitcast.38), kind=kOutput, calls=%fused_computation.40 | convolution fusion | flops 2147483648 | bytes 76546048 | tf_op jit(solution)/shard_map/fis,fjs->fij/dot_general | solution.py:48
  223.6 34.2 %fusion.1 = (f32[1,32,128,1024]{3,2,1,0:T(8,128)}, f32[1,32,128,1024]{3,2,1,0:T(8,128)}) fusion(f32[32,256,2048]{2,1,0:T(8,128)} %fusion.25), kind=kLoop, calls=%fused_computation.4 | loop fusion | flops 8388608 | bytes 100663296 | tf_op jit(solution)/shard_map/stack | solution.py:51
  257.8 24.7 %maximum_multiply_fusion = f32[2,32,128,1024]{3,2,1,0:T(8,128)} fusion(f32[1,32,128,1024]{3,2,1,0:T(8,128)} %get-tuple-element.6, f32[1,32,128,1024]{3,2,1,0:T(8,128)} %get-tuple-element.5), kind=kLoop, calls=%fused_computation | loop fusion | flops 16777216 | bytes 67108864 | tf_op jit(solution)/shard_map/div | solution.py:70
  (3 shorter events, 0.0 us)
Async XLA Ops:
  6.5 19.1 %copy-start = (s32[4,512]{1,0:T(4,128)S(1)}, s32[4,512]{1,0:T(4,128)}, u32[]{:S(2)}) copy-start(s32[4,512]{1,0:T(4,128)} %param.3) | copy-start | bytes 24580
  6.5 182.1 %all-gather.2.cloned.1.call-start = ((), (), s32[]{:S(2)}) async-start(), calls=%async_computation.1 | async-start | bytes 9437184 | tf_op jit(solution)/shard_map/all_gather | solution.py:69
  19.6 21.6 %collective-permute-start = (bf16[2,128,1536]{1,2,0:T(8,128)(2,1)S(1)}, bf16[2,128,1536]{1,2,0:T(8,128)(2,1)S(1)}, u32[]{:S(2)}, u32[]{:S(2)}) collective-permute-start(bf16[2,128,1536]{1,2,0:T(8,128)(2,1)S(1)} %slice.53), channel_id=1, source_target_pairs={{0,2},{1,3},{4,6},{5,7},{8,10},{9,11},{12,14},{13,15},{16,18},{17,... | collective-permute-start | bytes 2359304 | tf_op jit(solution)/shard_map/ppermute | solution.py:14
Sparse Core Ops, SparseCore 0:
  105.7 82.8 all-gather.1
where the time goes:
time: 290 us; the launch traced here: 289 us
  waiting for transfers between devices  96.8 us (33%)
  other arithmetic  83.3 us (29%)
  matrix products  48.9 us (17%)
  local copies, waits for them, and re-layouts  25.6 us (9%)
  blocking collectives  16.4 us (6%)
  between operations  13.5 us (5%)
  starting transfers between devices  4.89 us (2%)
    all_gather x1, waiting for transfers between devices, body(): lax.all_gather(turned, ('inp', 'pol'), axis=2, tiled=True)  81.2 us
    another operation x1, other arithmetic, accumulate(): update = jnp.stack([real_part, imag_part], axis=0)  34.2 us
    dot_general x1, matrix products, accumulate(): jnp.einsum('fis,fjs->fij', left_rows, right_rows, preferred_element_type=...  26.8 us
    div x1, other arithmetic, body(): return partial_value / (32.0 * turned.shape[3])  24.7 us
    dot_general x1, matrix products, body(): jnp.einsum('afbp,bisp->fais', dft_table(CHANNELS, points), filtered, pref...  22.1 us
    all_to_all x1, blocking collectives, body(): lax.all_to_all(spectra, 'slab', split_axis=0, concat_axis=3, tiled=True)  16.4 us
    ppermute x1, waiting for transfers between devices, passed_along(): lax.ppermute(value, axis, [(source, source + steps) for source in range(f...  15.6 us
    convert_element_type x1, other arithmetic, filter_bank(): extended = jnp.concatenate([tail_rows, voltage], axis=2).astype(jnp.float32)  12.8 us
  transfers between devices with their start and end apart: 2, of which 2 were waited for; matrix products, arithmetic and copies ran while one was open for 1% of the time, Pallas kernels for 0%

commit v1 on v0

--- a/solution.py
+++ b/solution.py
@@ -1,11 +1,18 @@
+import functools
 import math
 
 import jax
 import jax.numpy as jnp
+import numpy as np
 from jax import lax
+from jax.experimental import pallas as pl
+from jax.experimental.pallas import tpu as pltpu
 from jax.sharding import PartitionSpec as P
 
 CHANNELS = 64
+GROUP = 8
+LANES = 128
+MESH = pl.DeviceIdType.MESH
 
 
 def passed_along(value, axis, steps):
@@ -41,23 +48,7 @@
     return filtered.astype(jnp.bfloat16)
 
 
-def accumulate(left_rows, incoming):
-    row_count = left_rows.shape[1] // 2
-    col_count = incoming.shape[2]
-    right_rows = incoming.reshape(incoming.shape[0], 2 * col_count, incoming.shape[3])
-    products = jnp.einsum("fis,fjs->fij", left_rows, right_rows, preferred_element_type=jnp.float32)
-    real_part = products[:, :row_count, :col_count] + products[:, row_count:, col_count:]
-    imag_part = products[:, row_count:, :col_count] - products[:, :row_count, col_count:]
-    update = jnp.stack([real_part, imag_part], axis=0)
-    return update
-
-
-def make_step(turned, incoming):
-    left_rows = turned.reshape(turned.shape[0], 2 * turned.shape[2], turned.shape[3])
-    return accumulate(left_rows, incoming)
-
-
-def body(voltage, filter_taps):
+def general_body(voltage, filter_taps):
     points = filter_taps.shape[1]
     tail_length = (filter_taps.shape[0] - 1) * points
     tail_rows = passed_along(voltage[:, :, voltage.shape[2] - tail_length :], "slab", 1)
@@ -66,8 +57,360 @@
         "afbp,bisp->fais", dft_table(CHANNELS, points), filtered, preferred_element_type=jnp.float32
     ).astype(jnp.bfloat16)
     turned = lax.all_to_all(spectra, "slab", split_axis=0, concat_axis=3, tiled=True)
-    partial_value = make_step(turned, lax.all_gather(turned, ("inp", "pol"), axis=2, tiled=True))
-    return partial_value / (32.0 * turned.shape[3])
+    row_count = turned.shape[2]
+    left = turned.reshape(turned.shape[0], 2 * row_count, turned.shape[3])
+    incoming = lax.all_gather(turned, ("inp", "pol"), axis=2, tiled=True)
+    col_count = incoming.shape[2]
+    right = incoming.reshape(incoming.shape[0], 2 * col_count, incoming.shape[3])
+    products = jnp.einsum("fis,fjs->fij", left, right, preferred_element_type=jnp.float32)
+    real_part = products[:, :row_count, :col_count] + products[:, row_count:, col_count:]
+    imag_part = products[:, row_count:, :col_count] - products[:, :row_count, col_count:]
+    return jnp.stack([real_part, imag_part], axis=0) / (32.0 * turned.shape[3])
+
+
+def spectra_kernel(
+    depth, chunks, taps_ref, table_ref, volt_ref, g_ref,
+    ext, filt, ybuf, tbuf, stage, load_sem, tail_sem, local_sem, x_sem, send_sem, recv_sem,
+):
+    tap_count, points = taps_ref.shape
+    tail = (tap_count - 1) * points
+    span = GROUP * points
+    half = CHANNELS // 2
+    inputs = volt_ref.shape[1]
+    z = lax.axis_index("inp")
+    x = lax.axis_index("slab")
+    c = lax.axis_index("pol")
+    me = z * 2 + c
+    last = chunks - 1
+
+    barrier = pltpu.get_barrier_semaphore()
+    pl.semaphore_signal(barrier, inc=1, device_id={"pol": 1 - c}, device_id_type=MESH)
+    pl.semaphore_signal(barrier, inc=1, device_id={"slab": 1 - x}, device_id_type=MESH)
+
+    @pl.when(z > 0)
+    def _():
+        pl.semaphore_signal(barrier, inc=1, device_id={"inp": z - 1}, device_id_type=MESH)
+
+    @pl.when(z < depth - 1)
+    def _():
+        pl.semaphore_signal(barrier, inc=1, device_id={"inp": z + 1}, device_id_type=MESH)
+
+    below = jnp.where(z > 0, 1, 0)
+    above = jnp.where(z < depth - 1, 1, 0)
+    peers = 2 + below + above
+
+    def chunk_of(m):
+        return m + x * (last - 2 * m)
+
+    def load(n):
+        at = pl.multiple_of(chunk_of(n) * span, span)
+        return pltpu.make_async_copy(
+            volt_ref.at[:, :, pl.ds(at, span)],
+            ext.at[:, :, pl.ds(pl.multiple_of(at + tail, points), span)],
+            load_sem.at[n],
+        )
+
+    for n in range(chunks):
+        load(n).start()
+
+    @pl.when(x == 0)
+    def _():
+        ext[:, :, 0:tail] = jnp.zeros((2, inputs, tail), ext.dtype)
+
+    def tail_copy():
+        return pltpu.make_async_remote_copy(
+            src_ref=volt_ref.at[:, :, pl.ds(chunks * span - tail, tail)],
+            dst_ref=ext.at[:, :, pl.ds(0, tail)],
+            send_sem=tail_sem.at[0],
+            recv_sem=tail_sem.at[1],
+            device_id={"slab": 1 - x},
+            device_id_type=MESH,
+        )
+
+    def compute(m):
+        base = pl.multiple_of(chunk_of(m) * span, span)
+        wide = 256
+
+        for b in range(2):
+            for w in range(points // wide):
+                scale = [
+                    taps_ref[k : k + 1, w * wide : (w + 1) * wide].astype(jnp.float32)
+                    * (1.0 / 128.0)
+                    for k in range(tap_count)
+                ]
+
+                def rows(r, carry):
+                    row = pl.multiple_of(r * 16, 16)
+                    frames = []
+                    for s in range(GROUP + tap_count - 1):
+                        at = pl.multiple_of(base + s * points + w * wide, wide)
+                        frames.append(
+                            ext[b, pl.ds(row, 16), pl.ds(at, wide)].astype(jnp.float32)
+                        )
+                        if s >= tap_count - 1:
+                            first = s - tap_count + 1
+                            total = scale[0] * frames[first]
+                            for k in range(1, tap_count):
+                                total = total + scale[k] * frames[first + k]
+                            filt[
+                                pl.ds(pl.multiple_of(first * inputs + row, 16), 16),
+                                pl.ds(b * points + w * wide, wide),
+                            ] = total.astype(jnp.bfloat16)
+                    return carry
+
+                lax.fori_loop(0, inputs // 16, rows, 0)
+        ybuf[...] = jnp.dot(filt[...], table_ref[...], preferred_element_type=jnp.float32)
+        for s in range(GROUP):
+            tbuf[s * 2 * CHANNELS : (s + 1) * 2 * CHANNELS, :] = ybuf[
+                s * inputs : (s + 1) * inputs, :
+            ].T
+        for f in range(CHANNELS):
+            real = tbuf[pl.ds(f, GROUP, stride=2 * CHANNELS), :]
+            imag = tbuf[pl.ds(CHANNELS + f, GROUP, stride=2 * CHANNELS), :]
+            stage[m, f] = jnp.concatenate([real, imag], axis=0).astype(jnp.bfloat16)
+
+    def remote(src, q, dev, sem, where):
+        return pltpu.make_async_remote_copy(
+            src_ref=src,
+            dst_ref=g_ref.at[q, dev],
+            send_sem=sem,
+            recv_sem=recv_sem.at[q, dev],
+            device_id=where,
+            device_id_type=MESH,
+        )
+
+    def up(src, q, zs):
+        return remote(src, q, zs * 2 + c, send_sem.at[0, q, zs], {"inp": z + 1})
+
+    def down(src, q, zs):
+        return remote(src, q, zs * 2 + c, send_sem.at[1, q, zs], {"inp": z - 1})
+
+    def across(src, q, zs):
+        return remote(src, q, zs * 2 + c, send_sem.at[2, q, zs], {"pol": 1 - c})
+
+    def spread(src, q):
+        @pl.when(z < depth - 1)
+        def _():
+            up(src, q, z).start()
+
+        @pl.when(z > 0)
+        def _():
+            down(src, q, z).start()
+
+        across(src, q, z).start()
+
+    def mine(m):
+        return stage.at[m, pl.ds(pl.multiple_of(x * half, half), half)]
+
+    def theirs(m):
+        return stage.at[m, pl.ds(pl.multiple_of((1 - x) * half, half), half)]
+
+    def keep(m):
+        return pltpu.make_async_copy(mine(m), g_ref.at[x * chunks + m, me], local_sem.at[m])
+
+    def give(m):
+        return remote(theirs(m), x * chunks + m, me, x_sem.at[m], {"slab": 1 - x})
+
+    def send_own(m):
+        give(m).start()
+        spread(mine(m), x * chunks + m)
+        keep(m).start()
+
+    def send_given(m):
+        q = (1 - x) * chunks + m
+        slot = g_ref.at[q, me]
+        remote(slot, q, me, x_sem.at[m], {"slab": 1 - x}).wait_recv()
+        spread(slot, q)
+
+    def forward(q, distance):
+        @pl.when(z - distance >= 0)
+        def _():
+            zs = z - distance
+            slot = g_ref.at[q, zs * 2 + c]
+            up(slot, q, zs).wait_recv()
+
+            @pl.when(z < depth - 1)
+            def _():
+                up(slot, q, zs).start()
+
+            across(slot, q, zs).start()
+
+        @pl.when(z + distance < depth)
+        def _():
+            zs = z + distance
+            slot = g_ref.at[q, zs * 2 + c]
+            down(slot, q, zs).wait_recv()
+
+            @pl.when(z > 0)
+            def _():
+                down(slot, q, zs).start()
+
+            across(slot, q, zs).start()
+
+    load(0).wait()
+
+    def early(m, carry):
+        load(m + 1).wait()
+        compute(m)
+
+        @pl.when(m == 0)
+        def _():
+            pl.semaphore_wait(barrier, peers)
+
+        send_own(m)
+        return carry
+
+    lax.fori_loop(0, last, early, 0)
+
+    @pl.when(x == 0)
+    def _():
+        tail_copy().start()
+
+    for m in range(last):
+        send_given(m)
+
+    def forward_early(distance):
+        def step(m, carry):
+            forward(m, distance)
+            forward(chunks + m, distance)
+            return carry
+
+        lax.fori_loop(0, last, step, 0)
+
+    for distance in range(1, depth - 1):
+        forward_early(distance)
+
+    @pl.when(x == 1)
+    def _():
+        tail_copy().wait_recv()
+
+    compute(last)
+    send_own(last)
+    send_given(last)
+    for distance in range(1, depth - 1):
+        forward(last, distance)
+        forward(chunks + last, distance)
+    forward_early(depth - 1)
+    forward(last, depth - 1)
+    forward(chunks + last, depth - 1)
+
+    def finish(q, carry):
+        for zs in range(depth):
+            other = zs * 2 + 1 - c
+            remote(
+                g_ref.at[q, other], q, other, send_sem.at[2, q, zs], {"pol": 1 - c}
+            ).wait_recv()
+            slot = g_ref.at[q, zs * 2 + c]
+
+            @pl.when((z >= zs) & (z < depth - 1))
+            def _():
+                up(slot, q, zs).wait_send()
+
+            @pl.when((z <= zs) & (z > 0))
+            def _():
+                down(slot, q, zs).wait_send()
+
+            across(slot, q, zs).wait_send()
+        return carry
+
+    lax.fori_loop(0, 2 * chunks, finish, 0)
+    for m in range(chunks):
+        keep(m).wait()
+        give(m).wait_send()
+
+    @pl.when(x == 0)
+    def _():
+        tail_copy().wait_send()
+
+
+def correlate_kernel(spectra_total, g_ref, out_ref):
+    slots, devices, channels, rows, lanes = g_ref.shape
+    me = lax.axis_index("inp") * 2 + lax.axis_index("pol")
+    scale = 1.0 / (32.0 * spectra_total)
+    for f in range(channels):
+        own = g_ref[:, me, f].astype(jnp.float32) * scale
+        real, imag = own[:, : rows // 2], own[:, rows // 2 :]
+        straight = own.reshape(slots * rows, lanes).T
+        crossed = jnp.concatenate([imag, -real], axis=1).reshape(slots * rows, lanes).T
+        left = jnp.concatenate([straight, crossed], axis=0).astype(jnp.bfloat16)
+        right = jnp.concatenate(
+            [g_ref[:, j, f].reshape(slots * rows, lanes) for j in range(devices)], axis=1
+        )
+        product = jnp.dot(left, right, preferred_element_type=jnp.float32)
+        out_ref[0, f] = product[:lanes]
+        out_ref[1, f] = product[lanes:]
+
+
+def fast_body(voltage, filter_taps):
+    depth = lax.axis_size("inp")
+    tap_count, points = filter_taps.shape
+    inputs, samples = voltage.shape[1:]
+    chunks = samples // points // GROUP
+    half = CHANNELS // 2
+    devices = depth * 2
+    channel = np.arange(CHANNELS, dtype=np.int64)[:, None]
+    angles = (channel * np.arange(points)[None, :] % points).astype(np.float32)
+    angles = (angles * np.float32(2.0 * math.pi / points)).astype(np.float64)
+    cosine, sine = np.cos(angles) / 32.0, np.sin(angles) / 32.0
+    rows = np.concatenate(
+        [np.concatenate([cosine, sine], 1), np.concatenate([-sine, cosine], 1)], 0
+    )
+    table = jnp.asarray(rows.T.astype(np.float32)).astype(jnp.bfloat16)
+    vmem = pl.BlockSpec(memory_space=pltpu.VMEM)
+    hbm = pl.BlockSpec(memory_space=pl.ANY)
+    gathered = pl.pallas_call(
+        functools.partial(spectra_kernel, depth, chunks),
+        out_shape=jax.ShapeDtypeStruct(
+            (2 * chunks, devices, half, 2 * GROUP, LANES), jnp.bfloat16
+        ),
+        in_specs=[vmem, vmem, hbm],
+        out_specs=hbm,
+        scratch_shapes=[
+            pltpu.VMEM((2, inputs, samples + (tap_count - 1) * points), jnp.bfloat16),
+            pltpu.VMEM((GROUP * inputs, 2 * points), jnp.bfloat16),
+            pltpu.VMEM((GROUP * inputs, 2 * CHANNELS), jnp.float32),
+            pltpu.VMEM((GROUP * 2 * CHANNELS, inputs), jnp.float32),
+            pltpu.VMEM((chunks, CHANNELS, 2 * GROUP, inputs), jnp.bfloat16),
+            pltpu.SemaphoreType.DMA((chunks,)),
+            pltpu.SemaphoreType.DMA((2,)),
+            pltpu.SemaphoreType.DMA((chunks,)),
+            pltpu.SemaphoreType.DMA((chunks,)),
+            pltpu.SemaphoreType.DMA((3, 2 * chunks, depth)),
+            pltpu.SemaphoreType.DMA((2 * chunks, devices)),
+        ],
+        compiler_params=pltpu.CompilerParams(
+            collective_id=0, has_side_effects=True, vmem_limit_bytes=40 * 1024 * 1024
+        ),
+        name="spectra",
+    )(filter_taps, table, voltage)
+    step = 2
+    return pl.pallas_call(
+        functools.partial(correlate_kernel, 2 * chunks * GROUP),
+        grid=(half // step,),
+        out_shape=jax.ShapeDtypeStruct((2, half, inputs, devices * inputs), jnp.float32),
+        in_specs=[
+            pl.BlockSpec(
+                (2 * chunks, devices, step, 2 * GROUP, LANES), lambda f: (0, 0, f, 0, 0)
+            )
+        ],
+        out_specs=pl.BlockSpec((2, step, inputs, devices * inputs), lambda f: (0, f, 0, 0)),
+        compiler_params=pltpu.CompilerParams(vmem_limit_bytes=32 * 1024 * 1024),
+        name="correlate",
+    )(gathered)
+
+
+def body(voltage, filter_taps):
+    spectra_here = voltage.shape[2] // filter_taps.shape[1]
+    suits = (
+        lax.axis_size("slab") == 2
+        and lax.axis_size("pol") == 2
+        and voltage.shape[1] == LANES
+        and filter_taps.shape[1] % 256 == 0
+        and spectra_here % GROUP == 0
+        and spectra_here >= 2 * GROUP
+        and 1 < filter_taps.shape[0] <= GROUP + 1
+    )
+    return fast_body(voltage, filter_taps) if suits else general_body(voltage, filter_taps)
 
 
 def solution(mesh):

time: 290 us -> 95.8 us (0.33)
  waiting for transfers between devices: 96.8 us -> 0 us
  Pallas kernels: 0 us -> 94 us
  other arithmetic: 83.3 us -> 0 us
  matrix products: 48.9 us -> 0 us
  local copies, waits for them, and re-layouts: 25.6 us -> 1.65 us
  blocking collectives: 16.4 us -> 0 us
  between operations: 13.5 us -> 0.01 us
  starting transfers between devices: 4.89 us -> 0 us
    pallas_call x0 -> x2, Pallas kernels: none -> 94 us  [the longest x1 78.5 us: fast_body(): pl.pallas_call(functools.partial(spectra_kernel, depth, chunks), out_shap...]
    all_gather x1 -> x0, waiting for transfers between devices: 81.2 us -> none  [body(): lax.all_gather(turned, ('inp', 'pol'), axis=2, tiled=True)]
    dot_general x2 -> x0, matrix products: 48.9 us -> none  [the longest x1 26.8 us: accumulate(): jnp.einsum('fis,fjs->fij', left_rows, right_rows, preferred_element_type=...]
    another operation x4 -> x0, other arithmetic: 35.3 us -> none  [the longest x1 34.2 us: accumulate(): update = jnp.stack([real_part, imag_part], axis=0)]
    div x2 -> x0, other arithmetic: 24.7 us -> none  [the longest x1 24.7 us: body(): return partial_value / (32.0 * turned.shape[3])]
    all_to_all x1 -> x0, blocking collectives: 16.4 us -> none  [body(): lax.all_to_all(spectra, 'slab', split_axis=0, concat_axis=3, tiled=True)]
    ppermute x1 -> x0, waiting for transfers between devices: 15.6 us -> none  [passed_along(): lax.ppermute(value, axis, [(source, source + steps) for source in range(f...]
    convert_element_type x1 -> x0, other arithmetic: 12.8 us -> none  [filter_bank(): extended = jnp.concatenate([tail_rows, voltage], axis=2).astype(jnp.float32)]
  transfers between devices with their start and end apart: 2 -> 0, of which waited for: 2 -> 0; matrix products, arithmetic and copies ran while one was open for 1% -> 0% of each run, Pallas kernels for 0% -> 0%
where the time goes in v1:
time: 95.8 us; the launch traced here: 95.6 us
  Pallas kernels  94 us (98%)
  local copies, waits for them, and re-layouts  1.65 us (2%)
    pallas_call x1, Pallas kernels, fast_body(): pl.pallas_call(functools.partial(spectra_kernel, depth, chunks), out_shap...  78.5 us
    pallas_call x1, Pallas kernels, fast_body(): pl.pallas_call(functools.partial(correlate_kernel, 2 * chunks * GROUP), g...  15.5 us

profile of v1, /device:TPU:0, one launch (start us, length us, event | category | flops | bytes accessed | tf_op | source)
XLA Modules:
  0.0 95.6 jit_solution(15556945655023098718)
XLA Ops:
  0.0 0.0 copy-start
  0.0 0.9 copy-done
  1.0 0.0 copy-start.1
  1.0 0.7 copy-done.1
  1.6 78.5 %spectra.1.g_ref = bf16[8,8,32,16,128]{4,3,2,1,0:T(8,128)(2,1)S(1)} custom-call(s32[4,512]{1,0:T(4,128)S(1)} %copy-done.1, bf16[1024,128]{1,0:T(8,128)(2,1)S(1)} %copy-done, bf16[2,128,16384]{2,1,0:T(8,128)(2,1)} %volt_ref.1), custom_call_target="tpu_custom_call" | custom-call | tf_op jit(solution)/shard_map/spectra/pallas_call | solution.py:361
  80.2 15.5 %correlate.1 = f32[2,32,128,1024]{3,2,1,0:T(8,128)} custom-call(bf16[8,8,32,16,128]{4,3,2,1,0:T(8,128)(2,1)S(1)} %spectra.1.g_ref), custom_call_target="tpu_custom_call" | custom-call | tf_op jit(solution)/shard_map/correlate/pallas_call | solution.py:387
Async XLA Ops:
  0.0 0.9 copy-start
  1.0 0.7 copy-start.1

commit v2 on v1

--- a/solution.py
+++ b/solution.py
@@ -69,8 +69,8 @@
 
 
 def spectra_kernel(
-    depth, chunks, taps_ref, table_ref, volt_ref, g_ref,
-    ext, filt, ybuf, tbuf, stage, load_sem, tail_sem, local_sem, x_sem, send_sem, recv_sem,
+    depth, chunks, taps_hbm, table_hbm, volt_ref, g_ref,
+    taps_ref, table_ref, ext, filt, ybuf, tbuf, stage, aux_sem, load_sem, tail_sem, local_sem, x_sem, send_sem, recv_sem,
 ):
     tap_count, points = taps_ref.shape
     tail = (tap_count - 1) * points
@@ -102,16 +102,23 @@
     def chunk_of(m):
         return m + x * (last - 2 * m)
 
+    total_span = chunks * span
+
     def load(n):
-        at = pl.multiple_of(chunk_of(n) * span, span)
+        low = n * span + (tail if n else 0)
+        size = min(span + (0 if n else tail), total_span - low)
+        at = pl.multiple_of(low + x * (total_span - size - 2 * low), points)
         return pltpu.make_async_copy(
-            volt_ref.at[:, :, pl.ds(at, span)],
-            ext.at[:, :, pl.ds(pl.multiple_of(at + tail, points), span)],
+            volt_ref.at[:, :, pl.ds(at, size)],
+            ext.at[:, :, pl.ds(pl.multiple_of(at + tail, points), size)],
             load_sem.at[n],
         )
 
-    for n in range(chunks):
-        load(n).start()
+    taps_copy = pltpu.make_async_copy(taps_hbm, taps_ref, aux_sem.at[0])
+    table_copy = pltpu.make_async_copy(table_hbm, table_ref, aux_sem.at[1])
+    load(0).start()
+    taps_copy.start()
+    table_copy.start()
 
     @pl.when(x == 0)
     def _():
@@ -248,9 +255,12 @@
             across(slot, q, zs).start()
 
     load(0).wait()
+    for n in range(1, chunks):
+        load(n).start()
+    taps_copy.wait()
+    table_copy.wait()
 
     def early(m, carry):
-        load(m + 1).wait()
         compute(m)
 
         @pl.when(m == 0)
@@ -258,6 +268,12 @@
             pl.semaphore_wait(barrier, peers)
 
         send_own(m)
+        for n in range(1, chunks):
+
+            @pl.when(m == n - 1)
+            def _():
+                load(n).wait()
+
         return carry
 
     lax.fori_loop(0, last, early, 0)
@@ -290,44 +306,75 @@
     for distance in range(1, depth - 1):
         forward(last, distance)
         forward(chunks + last, distance)
+    def finish(q, zs):
+        other = zs * 2 + 1 - c
+        remote(
+            g_ref.at[q, other], q, other, send_sem.at[2, q, zs], {"pol": 1 - c}
+        ).wait_recv()
+        slot = g_ref.at[q, zs * 2 + c]
+
+        @pl.when((z >= zs) & (z < depth - 1))
+        def _():
+            up(slot, q, zs).wait_send()
+
+        @pl.when((z <= zs) & (z > 0))
+        def _():
+            down(slot, q, zs).wait_send()
+
+        across(slot, q, zs).wait_send()
+
+    def far(zs):
+        return (z - zs == depth - 1) | (zs - z == depth - 1)
+
+    def finish_near(q, carry):
+        for zs in range(depth):
+
+            @pl.when(jnp.logical_not(far(zs)))
+            def _():
+                finish(q, zs)
+
+        return carry
+
+    def finish_far(q, carry):
+        for zs in (0, depth - 1):
+
+            @pl.when(far(zs))
+            def _():
+                finish(q, zs)
+
+        return carry
+
+    lax.fori_loop(0, 2 * chunks, finish_near, 0)
+    for m in range(chunks):
+        keep(m).wait()
+        give(m).wait_send()
+
+    @pl.when(x == 0)
+    def _():
+        tail_copy().wait_send()
+
     forward_early(depth - 1)
     forward(last, depth - 1)
     forward(chunks + last, depth - 1)
-
-    def finish(q, carry):
-        for zs in range(depth):
-            other = zs * 2 + 1 - c
-            remote(
-                g_ref.at[q, other], q, other, send_sem.at[2, q, zs], {"pol": 1 - c}
-            ).wait_recv()
-            slot = g_ref.at[q, zs * 2 + c]
-
-            @pl.when((z >= zs) & (z < depth - 1))
-            def _():
-                up(slot, q, zs).wait_send()
-
-            @pl.when((z <= zs) & (z > 0))
-            def _():
-                down(slot, q, zs).wait_send()
-
-            across(slot, q, zs).wait_send()
-        return carry
-
-    lax.fori_loop(0, 2 * chunks, finish, 0)
-    for m in range(chunks):
-        keep(m).wait()
-        give(m).wait_send()
-
-    @pl.when(x == 0)
-    def _():
-        tail_copy().wait_send()
-
-
-def correlate_kernel(spectra_total, g_ref, out_ref):
+    lax.fori_loop(0, 2 * chunks, finish_far, 0)
+
+
+def correlate_kernel(spectra_total, g_ref, out_ref, buf, sem):
     slots, devices, channels, rows, lanes = g_ref.shape
+    depth = buf.shape[0]
     me = lax.axis_index("inp") * 2 + lax.axis_index("pol")
     scale = 1.0 / (32.0 * spectra_total)
-    for f in range(channels):
+
+    def put(f, slot):
+        return pltpu.make_async_copy(buf.at[slot], out_ref.at[:, f], sem.at[slot])
+
+    def step(f, carry):
+        slot = lax.rem(f, depth)
+
+        @pl.when(f >= depth)
+        def _():
+            put(f - depth, slot).wait()
+
         own = g_ref[:, me, f].astype(jnp.float32) * scale
         real, imag = own[:, : rows // 2], own[:, rows // 2 :]
         straight = own.reshape(slots * rows, lanes).T
@@ -337,8 +384,14 @@
             [g_ref[:, j, f].reshape(slots * rows, lanes) for j in range(devices)], axis=1
         )
         product = jnp.dot(left, right, preferred_element_type=jnp.float32)
-        out_ref[0, f] = product[:lanes]
-        out_ref[1, f] = product[lanes:]
+        buf[slot, 0] = product[:lanes]
+        buf[slot, 1] = product[lanes:]
+        put(f, slot).start()
+        return carry
+
+    lax.fori_loop(0, channels, step, 0)
+    for f in range(channels - depth, channels):
+        put(f, f % depth).wait()
 
 
 def fast_body(voltage, filter_taps):
@@ -360,17 +413,18 @@
     hbm = pl.BlockSpec(memory_space=pl.ANY)
     gathered = pl.pallas_call(
         functools.partial(spectra_kernel, depth, chunks),
-        out_shape=jax.ShapeDtypeStruct(
-            (2 * chunks, devices, half, 2 * GROUP, LANES), jnp.bfloat16
-        ),
-        in_specs=[vmem, vmem, hbm],
-        out_specs=hbm,
+        out_shape=pltpu.VMEM((2 * chunks, devices, half, 2 * GROUP, LANES), jnp.bfloat16),
+        in_specs=[pl.BlockSpec(memory_space=pltpu.HBM)] * 3,
+        out_specs=vmem,
         scratch_shapes=[
+            pltpu.VMEM((tap_count, points), jnp.int32),
+            pltpu.VMEM((2 * points, 2 * CHANNELS), jnp.bfloat16),
             pltpu.VMEM((2, inputs, samples + (tap_count - 1) * points), jnp.bfloat16),
             pltpu.VMEM((GROUP * inputs, 2 * points), jnp.bfloat16),
             pltpu.VMEM((GROUP * inputs, 2 * CHANNELS), jnp.float32),
             pltpu.VMEM((GROUP * 2 * CHANNELS, inputs), jnp.float32),
             pltpu.VMEM((chunks, CHANNELS, 2 * GROUP, inputs), jnp.bfloat16),
+            pltpu.SemaphoreType.DMA((2,)),
             pltpu.SemaphoreType.DMA((chunks,)),
             pltpu.SemaphoreType.DMA((2,)),
             pltpu.SemaphoreType.DMA((chunks,)),
@@ -382,19 +436,18 @@
             collective_id=0, has_side_effects=True, vmem_limit_bytes=40 * 1024 * 1024
         ),
         name="spectra",
-    )(filter_taps, table, voltage)
-    step = 2
+    )(*(pltpu.with_memory_space_constraint(a, pltpu.HBM) for a in (filter_taps, table, voltage)))
+    buffers = 4
     return pl.pallas_call(
         functools.partial(correlate_kernel, 2 * chunks * GROUP),
-        grid=(half // step,),
         out_shape=jax.ShapeDtypeStruct((2, half, inputs, devices * inputs), jnp.float32),
-        in_specs=[
-            pl.BlockSpec(
-                (2 * chunks, devices, step, 2 * GROUP, LANES), lambda f: (0, 0, f, 0, 0)
-            )
+        in_specs=[vmem],
+        out_specs=hbm,
+        scratch_shapes=[
+            pltpu.VMEM((buffers, 2, inputs, devices * inputs), jnp.float32),
+            pltpu.SemaphoreType.DMA((buffers,)),
         ],
-        out_specs=pl.BlockSpec((2, step, inputs, devices * inputs), lambda f: (0, f, 0, 0)),
-        compiler_params=pltpu.CompilerParams(vmem_limit_bytes=32 * 1024 * 1024),
+        compiler_params=pltpu.CompilerParams(vmem_limit_bytes=20 * 1024 * 1024),
         name="correlate",
     )(gathered)
 

time: 95.8 us -> 90.1 us (0.941)
  Pallas kernels: 94 us -> 89.9 us
  local copies, waits for them, and re-layouts: 1.65 us -> 0 us
    pallas_call x1, Pallas kernels: 15.5 us -> 11.8 us  [fast_body(): pl.pallas_call(functools.partial(correlate_kernel, 2 * chunks * GROUP), o...]
    unnamed x4 -> x0, local copies, waits for them, and re-layouts: 1.65 us -> none
where the time goes in v2:
time: 90.1 us; the launch traced here: 89.9 us
  Pallas kernels  89.9 us (100%)
    pallas_call x1, Pallas kernels, fast_body(): pl.pallas_call(functools.partial(spectra_kernel, depth, chunks), out_shap...  78.1 us
    pallas_call x1, Pallas kernels, fast_body(): pl.pallas_call(functools.partial(correlate_kernel, 2 * chunks * GROUP), o...  11.8 us

profile of v2, /device:TPU:0, one launch (start us, length us, event | category | flops | bytes accessed | tf_op | source)
XLA Modules:
  0.0 89.9 jit_solution(12805428367296759565)
XLA Ops:
  0.0 78.1 %spectra.1.g_ref = bf16[8,8,32,16,128]{4,3,2,1,0:T(8,128)(2,1)S(1)} custom-call(s32[4,512]{1,0:T(4,128)} %taps_hbm.1, bf16[1024,128]{1,0:T(8,128)(2,1)} %constant.3.table_hbm, bf16[2,128,16384]{2,1,0:T(8,128)(2,1)} %volt_ref.1), custom_call_target="tpu_custom_call" | custom-call | tf_op jit(solution)/shard_map/spectra/pallas_call | solution.py:414
  78.1 11.8 %correlate.1 = f32[2,32,128,1024]{3,2,1,0:T(8,128)} custom-call(bf16[8,8,32,16,128]{4,3,2,1,0:T(8,128)(2,1)S(1)} %spectra.1.g_ref), custom_call_target="tpu_custom_call" | custom-call | tf_op jit(solution)/shard_map/correlate/pallas_call | solution.py:441

commit v3 on v2

--- a/solution.py
+++ b/solution.py
@@ -116,8 +116,18 @@
 
     taps_copy = pltpu.make_async_copy(taps_hbm, taps_ref, aux_sem.at[0])
     table_copy = pltpu.make_async_copy(table_hbm, table_ref, aux_sem.at[1])
-    load(0).start()
+    def first_load(b):
+        size = span + tail
+        at = pl.multiple_of(x * (total_span - size), points)
+        return pltpu.make_async_copy(
+            volt_ref.at[b, :, pl.ds(at, size)],
+            ext.at[b, :, pl.ds(pl.multiple_of(at + tail, points), size)],
+            aux_sem.at[2 + b],
+        )
+
+    first_load(0).start()
     taps_copy.start()
+    first_load(1).start()
     table_copy.start()
 
     @pl.when(x == 0)
@@ -139,6 +149,16 @@
         wide = 256
 
         for b in range(2):
+            if not isinstance(m, int):
+
+                @pl.when(m == 0)
+                def _():
+                    first_load(b).wait()
+                    if b == 1:
+                        for n in range(1, chunks):
+                            load(n).start()
+                        table_copy.wait()
+
             for w in range(points // wide):
                 scale = [
                     taps_ref[k : k + 1, w * wide : (w + 1) * wide].astype(jnp.float32)
@@ -219,8 +239,8 @@
         return remote(theirs(m), x * chunks + m, me, x_sem.at[m], {"slab": 1 - x})
 
     def send_own(m):
+        spread(mine(m), x * chunks + m)
         give(m).start()
-        spread(mine(m), x * chunks + m)
         keep(m).start()
 
     def send_given(m):
@@ -254,11 +274,7 @@
 
             across(slot, q, zs).start()
 
-    load(0).wait()
-    for n in range(1, chunks):
-        load(n).start()
     taps_copy.wait()
-    table_copy.wait()
 
     def early(m, carry):
         compute(m)
@@ -424,7 +440,7 @@
             pltpu.VMEM((GROUP * inputs, 2 * CHANNELS), jnp.float32),
             pltpu.VMEM((GROUP * 2 * CHANNELS, inputs), jnp.float32),
             pltpu.VMEM((chunks, CHANNELS, 2 * GROUP, inputs), jnp.bfloat16),
-            pltpu.SemaphoreType.DMA((2,)),
+            pltpu.SemaphoreType.DMA((4,)),
             pltpu.SemaphoreType.DMA((chunks,)),
             pltpu.SemaphoreType.DMA((2,)),
             pltpu.SemaphoreType.DMA((chunks,)),

time: 90.1 us -> 89.7 us (level)
  no operation moved by 1% of the time
where the time goes in v3:
time: 89.7 us; the launch traced here: 89.5 us
  Pallas kernels  89.5 us (100%)
    pallas_call x1, Pallas kernels, fast_body(): pl.pallas_call(functools.partial(spectra_kernel, depth, chunks), out_shap...  77.7 us
    pallas_call x1, Pallas kernels, fast_body(): pl.pallas_call(functools.partial(correlate_kernel, 2 * chunks * GROUP), o...  11.8 us

profile of v3, /device:TPU:0, one launch (start us, length us, event | category | flops | bytes accessed | tf_op | source)
XLA Modules:
  0.0 89.5 jit_solution(7110013407637027087)
XLA Ops:
  0.0 77.7 %spectra.1.g_ref = bf16[8,8,32,16,128]{4,3,2,1,0:T(8,128)(2,1)S(1)} custom-call(s32[4,512]{1,0:T(4,128)} %taps_hbm.1, bf16[1024,128]{1,0:T(8,128)(2,1)} %constant.3.table_hbm, bf16[2,128,16384]{2,1,0:T(8,128)(2,1)} %volt_ref.1), custom_call_target="tpu_custom_call" | custom-call | tf_op jit(solution)/shard_map/spectra/pallas_call | solution.py:430
  77.7 11.8 %correlate.1 = f32[2,32,128,1024]{3,2,1,0:T(8,128)} custom-call(bf16[8,8,32,16,128]{4,3,2,1,0:T(8,128)(2,1)S(1)} %spectra.1.g_ref), custom_call_target="tpu_custom_call" | custom-call | tf_op jit(solution)/shard_map/correlate/pallas_call | solution.py:457
